TPU v7x, 32 devices: a whole 2x2x4 slice. The times are simulated.
32 devices in a mesh: groups: 2 (over y), ctx: 4 (over z), tp: 4 (over x, core).
Axes of the slice: x: 2, y: 2, z: 4, core: 2. Of those that a mesh axis runs over, the one named last changes fastest.
Arguments:
- q_in: bfloat16 [1024, 8192], P(('groups', 'ctx'), 'tp'), parts along dimension 0, may hold values from -6 to 6
- k_in: bfloat16 [1024, 8192], P(('groups', 'ctx'), 'tp'), parts along dimension 0, may hold values from -6 to 6
- v_in: bfloat16 [1024, 8192], P(('groups', 'ctx'), 'tp'), parts along dimension 0, may hold values from -6 to 6
- short_filters: float32 [3, 512, 7], P(None, 'tp'), may hold values from -2.5 to 2.5
- rates: float32 [16, 8192], P(None, 'tp'), may hold values from 1.953125e-05 to 0.0625
- residues: float32 [16, 8192], P(None, 'tp'), may hold values from -2.5 to 2.5
- out_weight: bfloat16 [8192, 4096], P('tp', 'ctx'), may hold values from -0.0625 to 0.0625
- cotangent: bfloat16 [1024, 4096], P(('groups', 'ctx'), 'tp'), parts along dimension 0, may hold values from -6 to 6
Outputs:
- out: bfloat16 [1024, 4096], P(('groups', 'ctx'), 'tp'), parts along dimension 0
- grad_q: bfloat16 [1024, 8192], P(('groups', 'ctx'), 'tp'), parts along dimension 0
- grad_k: bfloat16 [1024, 8192], P(('groups', 'ctx'), 'tp'), parts along dimension 0
- grad_v: bfloat16 [1024, 8192], P(('groups', 'ctx'), 'tp'), parts along dimension 0
- grad_short: float32 [6, 512, 7], P('groups', 'tp'), parts along dimension 0
There are 2 independent parts, one for each index of `groups`. A program takes and returns all parts, laid end to end along the dimension named above; an argument that names none is the same for every part. Nothing has to cross between parts.
All inputs are finite; a program needn't handle non-finite values.
Results may differ from a plain program's by a relative error of at most 0.013.
Values may be sent and summed in bfloat16 or wider, within the bound.
A program may use at most 192 MiB of HBM per device.

v0:
```python
import jax
import jax.numpy as jnp
from jax import lax
from jax.sharding import PartitionSpec as P

block_rows = 16


def shifted(shard, axis, by):
    length = lax.axis_size(axis)
    pairs = [(i, i + by) for i in range(length) if 0 <= i + by < length]
    return lax.ppermute(shard, axis, pairs)


def entering(shard, axis, combine, identity, reverse):
    length, index = (lax.axis_size(axis), lax.axis_index(axis))
    everything = jax.tree.map(
        lambda part, kind: lax.all_gather(part.astype(kind), axis),
        shard,
        (jnp.bfloat16, jnp.bfloat16),
    )
    start = jax.tree.map(
        lambda part, zero: jnp.broadcast_to(jnp.asarray(zero, part.dtype), part.shape),
        shard,
        identity,
    )

    def lap(k, before):
        at = length - 1 - k if reverse else k
        reached = at > index if reverse else at < index
        new = combine(
            before, jax.tree.map(lambda part, own: part[at].astype(own.dtype), everything, shard)
        )
        return jax.tree.map(lambda a, b: jnp.where(reached, a, b), new, before)

    return lax.fori_loop(0, length, lap, start)


def shortened(shard):
    return jax.tree.map(lambda a: a.astype(jnp.bfloat16) if a.dtype == jnp.float32 else a, shard)


def chain_link(earlier, following):
    return (earlier[0] * following[0], following[0] * earlier[1] + following[1])


def shards(q_in, k_in, v_in, short_filters, rates, residues, out_weight, cotangent):
    length, channels = q_in.shape
    filter_taps = short_filters.shape[2]
    group_count = short_filters.shape[1]
    group_size = channels // group_count
    blocks = length // block_rows
    sequence = length * lax.axis_size("ctx")
    highest = lax.Precision.HIGHEST
    stacked = jnp.stack([q_in, k_in, v_in])
    front_rows = shifted(stacked[:, length - filter_taps + 1 :, :], "ctx", 1)
    extended = jnp.concatenate([front_rows, stacked], axis=1).astype(jnp.float32)
    filter_rows = jnp.repeat(short_filters, group_size, axis=1)
    convolved = jnp.zeros((3, length, channels), jnp.float32)
    for shift_by in range(filter_taps):
        start = filter_taps - 1 - shift_by
        convolved = (
            convolved + filter_rows[:, None, :, shift_by] * extended[:, start : start + length, :]
        )
    query_conv = convolved[0]
    key_conv = convolved[1]
    value_conv = convolved[2]
    gated = key_conv * value_conv
    offsets = jnp.arange(block_rows, dtype=jnp.float32)
    scaled = residues * jnp.sqrt(-jnp.expm1(-2.0 * rates))
    powers = jnp.exp(-rates[None] * offsets[:, None, None])
    kernel = jnp.sum(powers * scaled[None], axis=1)
    lag_table = (
        jnp.arange(block_rows, dtype=jnp.int32)[:, None]
        - jnp.arange(block_rows, dtype=jnp.int32)[None, :]
    )
    toeplitz = jnp.where((lag_table >= 0)[:, :, None], kernel[jnp.maximum(lag_table, 0)], 0.0)
    end_powers = jnp.exp(-rates[None] * (block_rows - 1.0 - offsets)[:, None, None])
    lead_powers = scaled[None] * jnp.exp(-rates[None] * (offsets + 1.0)[:, None, None])
    tail_powers = scaled[None] * jnp.exp(-rates[None] * (block_rows - offsets)[:, None, None])
    block_index = jnp.arange(blocks, dtype=jnp.float32)
    block_decay = jnp.broadcast_to(jnp.exp(-rates * block_rows)[None], (blocks,) + rates.shape)
    entry_decay = jnp.exp(-rates[None] * (block_rows * block_index)[:, None, None])
    exit_decay = jnp.exp(-rates[None] * (block_rows * (blocks - 1.0 - block_index))[:, None, None])
    piece_decay = jnp.exp(-rates * length)
    identity = (jnp.ones_like(rates), jnp.zeros_like(rates))
    gated_blocks = gated.reshape(blocks, block_rows, channels)
    block_states = jnp.einsum("snc,bsc->bnc", end_powers, gated_blocks, precision=highest)
    prefix = lax.associative_scan(chain_link, (block_decay, block_states), axis=0)[1]
    local_end = prefix[-1]
    state_in = entering((piece_decay, local_end), "ctx", chain_link, identity, False)[1]
    earlier_states = jnp.concatenate([jnp.zeros_like(prefix[:1]), prefix[:-1]], axis=0)
    entry_states = earlier_states + entry_decay * state_in[None]
    mixed = jnp.einsum("tsc,bsc->btc", toeplitz, gated_blocks, precision=highest)
    mixed = mixed + jnp.einsum("tnc,bnc->btc", lead_powers, entry_states, precision=highest)
    mixed = mixed.reshape(length, channels)
    product = (query_conv * mixed).astype(jnp.bfloat16)
    weights = lax.all_gather(out_weight, "ctx", axis=1, tiled=True)
    partial_value = jnp.dot(product, weights, preferred_element_type=jnp.float32)
    output = lax.psum_scatter(
        partial_value.astype(jnp.bfloat16), "tp", scatter_dimension=1, tiled=True
    )
    seed = lax.all_gather(cotangent, "tp", axis=1, tiled=True)
    grad_product = lax.dot_general(
        seed, weights, (((1,), (1,)), ((), ())), preferred_element_type=jnp.float32
    )
    grad_query = grad_product * mixed
    grad_mixed = (grad_product * query_conv).reshape(blocks, block_rows, channels)
    block_adjoint = jnp.einsum("snc,bsc->bnc", powers, grad_mixed, precision=highest)
    suffix = lax.associative_scan(chain_link, (block_decay, block_adjoint), reverse=True, axis=0)[1]
    local_begin = suffix[0]
    adjoint_in = entering((piece_decay, local_begin), "ctx", chain_link, identity, True)[1]
    later_adjoint = jnp.concatenate([suffix[1:], jnp.zeros_like(suffix[:1])], axis=0)
    exit_adjoint = later_adjoint + exit_decay * adjoint_in[None]
    grad_gated = jnp.einsum("tsc,btc->bsc", toeplitz, grad_mixed, precision=highest)
    grad_gated = grad_gated + jnp.einsum(
        "snc,bnc->bsc", tail_powers, exit_adjoint, precision=highest
    )
    grad_gated = grad_gated.reshape(length, channels)
    grads = jnp.stack([grad_query, grad_gated * value_conv, grad_gated * key_conv])
    back_rows = shifted(shortened(grads[:, : filter_taps - 1, :]), "ctx", -1)
    grad_extended = jnp.concatenate([grads, back_rows], axis=1)
    input_grads = jnp.zeros((3, length, channels), jnp.float32)
    filter_terms = []
    for shift_by in range(filter_taps):
        input_grads = (
            input_grads
            + filter_rows[:, None, :, shift_by] * grad_extended[:, shift_by : shift_by + length, :]
        )
        start = filter_taps - 1 - shift_by
        filter_terms.append(jnp.sum(grads * extended[:, start : start + length, :], axis=1))
    local_filter = jnp.stack(filter_terms, axis=1)
    local_filter = (
        jnp.sum(local_filter.reshape(3, filter_taps, group_count, group_size), axis=3) / sequence
    )
    local_filter = jnp.transpose(local_filter, (0, 2, 1))
    grad_short = lax.psum(local_filter, "ctx")
    input_grads = input_grads.astype(jnp.bfloat16)
    return (output, input_grads[0], input_grads[1], input_grads[2], grad_short)


def solution(mesh):
    placed = (
        P(("groups", "ctx"), "tp"),
        P(("groups", "ctx"), "tp"),
        P(("groups", "ctx"), "tp"),
        P(None, "tp", None),
        P(None, "tp"),
        P(None, "tp"),
        P("tp", "ctx"),
        P(("groups", "ctx"), "tp"),
    )
    return jax.shard_map(
        shards,
        mesh=mesh,
        in_specs=placed,
        out_specs=(
            P(("groups", "ctx"), "tp"),
            P(("groups", "ctx"), "tp"),
            P(("groups", "ctx"), "tp"),
            P(("groups", "ctx"), "tp"),
            P("groups", "tp", None),
        ),
        check_vma=False,
    )
```

profile of v0, /device:TPU:0, one launch (start us, length us, event | category | flops | bytes accessed | tf_op | source)
XLA Modules:
  0.0 710.6 jit_solution(17691926385368568895)
XLA Ops:
  9.4 5.6 collective-permute-start
  17.9 4.8 multiply_reduce_fusion
  25.8 11.2 %copy.118 = f32[16,16,2048]{1,0,2:T(8,128)} copy(f32[16,16,2048]{2,1,0:T(8,128)S(1)} %bitcast.100) | data formatting | bytes 4194304 | tf_op jit(solution)/shard_map/gather | solution.py:77
  38.3 18.1 %all-gather = bf16[64,2048]{1,0:T(8,128)(2,1)} all-gather(bf16[16,2048]{1,0:T(8,128)(2,1)S(1)} %get-tuple-element.366), channel_id=2, replica_groups=mesh['groups'=2,'ctx'=4,'tp'=4] {'ctx'}, dimensions={0}, use_global_device_ids=true | all-gather | bytes 327680 | tf_op jit(solution)/shard_map/all_gather | solution.py:18
  58.3 4.1 multiply_add_fusion
  62.4 257.0 %all-gather.4.cloned.1.call-done = bf16[2048,4096]{1,0:T(8,128)(2,1)} async-done(((bf16[2048,1024]{1,0:T(8,128)(2,1)}), bf16[2048,4096]{1,0:T(8,128)(2,1)}) %all-gather.4.cloned.1.call-update) | async-done | bytes 16777232 | tf_op jit(solution)/shard_map/all_gather | solution.py:98
  319.4 13.3 %fusion.43 = (f32[128,2048]{1,0:T(8,128)}, f32[128,2048]{1,0:T(8,128)}) fusion(f32[3,128,2048]{2,1,0:T(8,128)} %multiply_add_fusion, bf16[128,4096]{1,0:T(8,128)(2,1)} %all-gather.6.cloned.1.call-done, bf16[2048,4096]{1,0:T(8,128)(2,1)} %all-gather.4.cloned.1.call-done), kind=kOutput, calls=%fused_computation.73 | convolution fusion | flops 2147745792 | bytes 20971520 | tf_op jit(solution)/shard_map/dot_general | solution.py:104
  332.7 6.0 copy.124
  338.7 19.6 %fusion.13 = f32[2048,8,16]{2,1,0:T(8,128)} fusion(f32[8,16,2048]{1,0,2:T(8,128)} %copy.124, f32[16,2048]{0,1:T(8,128)} %copy-done), kind=kOutput, calls=%fused_computation.20 | convolution fusion | flops 50855936 | bytes 2228224 | tf_op jit(solution)/shard_map/snc,bsc->bnc/dot_general | solution.py:109
  358.3 6.5 copy.126
  378.2 4.1 pad.184
  382.2 4.1 pad.51
  390.4 4.1 pad.50
  395.4 15.0 %all_gather.27 = bf16[4,16,2048]{2,1,0:T(8,128)(2,1)} all-gather(bf16[1,16,2048]{2,1,0:T(8,128)(2,1)S(1)} %add_convert_fusion), channel_id=1, replica_groups=mesh['groups'=2,'ctx'=4,'tp'=4] {'ctx'}, dimensions={0}, use_global_device_ids=true | all-gather | bytes 327680 | tf_op jit(solution)/shard_map/all_gather | solution.py:18
  410.5 3.9 while.31
  421.5 6.0 copy.127
  427.5 30.3 %fusion.2 = f32[2048,8,16]{2,1,0:T(8,128)S(1)} fusion(f32[8,16,2048]{1,0,2:T(8,128)} %copy.127, f32[16]{0:T(128)S(1)} %iota_subtract_fusion, f32[16,2048]{0,1:T(8,128)} %copy-done.1, f32[16,2048]{0,1:T(8,128)} %copy-done), kind=kOutput, calls=%fused_computation.7 | convolution fusion | flops 51380224 | bytes 2359360 | tf_op jit(solution)/shard_map/snc,bnc->bsc/dot_general | solution.py:116
  457.8 20.0 %add_bitcast_fusion = f32[8,16,2048]{1,0,2:T(8,128)} fusion(f32[2048,8,16]{2,1,0:T(8,128)S(1)} %fusion.2, f32[8,16,2048]{1,0,2:T(8,128)} %copy.124, f32[16,16,2048]{1,0,2:T(8,128)} %copy.118, pred[16,16]{1,0:T(8,128)(4,1)S(1)} %subtract_compare_fusion), kind=kOutput, calls=%fused_computation.25 | convolution fusion | flops 51118080 | bytes 5243136 | tf_op jit(solution)/shard_map/tsc,btc->bsc/dot_general | solution.py:115
  477.8 6.0 copy.128
  487.5 6.0 copy.119
  493.5 19.7 %fusion.10 = f32[2048,8,16]{2,1,0:T(8,128)} fusion(f32[8,16,2048]{1,0,2:T(8,128)} %copy.119, f32[16]{0:T(128)S(1)} %iota_subtract_fusion.1, f32[16,2048]{0,1:T(8,128)} %copy-done), kind=kOutput, calls=%fused_computation.15 | convolution fusion | flops 50855936 | bytes 2228288 | tf_op jit(solution)/shard_map/snc,bsc->bnc/dot_general | solution.py:88
  513.2 6.0 copy.121
  534.7 4.1 pad.182
  538.7 4.1 pad.45
  544.7 4.1 pad.44
  549.8 14.5 %all_gather.24 = bf16[4,16,2048]{2,1,0:T(8,128)(2,1)} all-gather(bf16[1,16,2048]{2,1,0:T(8,128)(2,1)S(1)} %add_convert_fusion.1), channel_id=1, replica_groups=mesh['groups'=2,'ctx'=4,'tp'=4] {'ctx'}, dimensions={0}, use_global_device_ids=true | all-gather | bytes 327680 | tf_op jit(solution)/shard_map/all_gather | solution.py:18
  564.3 3.9 while.30
  571.9 6.0 copy.122
  577.9 30.3 %fusion.6 = f32[2048,8,16]{2,1,0:T(8,128)S(1)} fusion(f32[8,16,2048]{1,0,2:T(8,128)} %copy.122, f32[16]{0:T(128)S(1)} %iota_add_fusion, f32[16,2048]{0,1:T(8,128)} %copy-done.1, f32[16,2048]{0,1:T(8,128)} %copy-done), kind=kOutput, calls=%fused_computation.11 | convolution fusion | flops 51380224 | bytes 2359360 | tf_op jit(solution)/shard_map/tnc,bnc->btc/dot_general | solution.py:95
  608.3 32.0 %add_bitcast_fusion.1 = f32[8,16,2048]{1,0,2:T(8,128)} fusion(f32[2048,8,16]{2,1,0:T(8,128)S(1)} %fusion.6, f32[8,16,2048]{1,0,2:T(8,128)} %copy.119, f32[16,16,2048]{1,0,2:T(8,128)} %copy.118, pred[16,16]{1,0:T(8,128)(4,1)S(1)} %subtract_compare_fusion), kind=kOutput, calls=%fused_computation.27 | convolution fusion | flops 51118080 | bytes 5243136 | tf_op jit(solution)/shard_map/tsc,bsc->btc/dot_general | solution.py:94
  640.3 6.0 copy.123
  680.4 18.2 %psum.7 = f32[3,128,7]{1,0,2:T(4,128)S(1)} all-reduce(f32[3,128,7]{1,0,2:T(4,128)S(1)} %multiply_bitcast_fusion), channel_id=1, replica_groups=mesh['groups'=2,'ctx'=4,'tp'=4] {'ctx'}, use_global_device_ids=true, to_apply=%region_14.15 | all-reduce | flops 2688 | bytes 21504 | tf_op jit(solution)/shard_map/psum | solution.py:137
  (187 shorter events, 108.9 us)
Async XLA Ops:
  7.2 7.9 %copy-start.16 = (f32[16,2048]{1,0:T(8,128)S(1)}, f32[16,2048]{1,0:T(8,128)}, u32[]{:S(2)}) copy-start(f32[16,2048]{1,0:T(8,128)} %param.16) | copy-start | bytes 393220
  7.2 7.9 %copy-start.32 = (f32[16,2048]{1,0:T(8,128)S(1)}, f32[16,2048]{1,0:T(8,128)}, u32[]{:S(2)}) copy-start(f32[16,2048]{1,0:T(8,128)} %param.17) | copy-start | bytes 393220
  7.2 55.2 %all-gather.6.cloned.1.call-start = ((), (), s32[]{:S(2)}) async-start(), calls=%async_computation.3 | async-start | bytes 1310720 | tf_op jit(solution)/shard_map/all_gather | solution.py:103
  8.0 311.4 %all-gather.4.cloned.1.call-start = ((), (), s32[]{:S(2)}) async-start(), calls=%async_computation.1 | async-start | bytes 20971520 | tf_op jit(solution)/shard_map/all_gather | solution.py:98
  8.7 695.2 %reduce-scatter.2.cloned.1.call-start = ((), (), s32[]{:S(2)}) async-start(), calls=%async_computation.2 | async-start | bytes 1310720 | tf_op jit(solution)/shard_map/reduce_scatter | solution.py:100
  9.4 46.9 %collective-permute-start = (bf16[3,6,2048]{2,1,0:T(8,128)(2,1)}, bf16[3,6,2048]{2,1,0:T(8,128)(2,1)}, u32[]{:S(2)}, u32[]{:S(2)}) collective-permute-start(bf16[3,6,2048]{2,1,0:T(8,128)(2,1)} %pad_maximum_fusion.6), channel_id=1, source_target_pairs={{0,4},{4,8},{8,12},{1,5},{5,9},{9,13},{2,6},{6,10},{10,14},{3,7},{... | collective-permute-start | bytes 221192 | tf_op jit(solution)/shard_map/ppermute | solution.py:12
  15.9 7.0 copy-start.33
  16.3 7.1 %copy-start.1 = (f32[16,2048]{0,1:T(8,128)}, f32[16,2048]{0,1:T(8,128)S(1)}, u32[]{:S(2)}) copy-start(f32[16,2048]{0,1:T(8,128)S(1)} %copy.116) | copy-start | bytes 393220
  24.3 33.9 %copy-start.18 = (f32[3,2048,1]{1,0,2:T(4,128)}, f32[3,2048,1]{1,0,2:T(4,128)S(1)}, u32[]{:S(2)}) copy-start(f32[3,2048,1]{1,0,2:T(4,128)S(1)} %copy.144) | copy-start | bytes 73732
  38.1 20.1 %copy-start.20 = (f32[3,2048]{1,0:T(4,128)}, f32[3,2048]{1,0:T(4,128)S(1)}, u32[]{:S(2)}) copy-start(f32[3,2048]{1,0:T(4,128)S(1)} %get-tuple-element.371) | copy-start | bytes 73732
  38.1 20.1 %copy-start.22 = (f32[3,2048]{1,0:T(4,128)}, f32[3,2048]{1,0:T(4,128)S(1)}, u32[]{:S(2)}) copy-start(f32[3,2048]{1,0:T(4,128)S(1)} %get-tuple-element.372) | copy-start | bytes 73732
  38.2 20.1 %copy-start.24 = (f32[3,2048]{1,0:T(4,128)}, f32[3,2048]{1,0:T(4,128)S(1)}, u32[]{:S(2)}) copy-start(f32[3,2048]{1,0:T(4,128)S(1)} %get-tuple-element.373) | copy-start | bytes 73732
  38.2 20.1 %copy-start.26 = (f32[3,2048]{1,0:T(4,128)}, f32[3,2048]{1,0:T(4,128)S(1)}, u32[]{:S(2)}) copy-start(f32[3,2048]{1,0:T(4,128)S(1)} %get-tuple-element.374) | copy-start | bytes 73732
  38.2 20.1 %copy-start.28 = (f32[3,2048]{1,0:T(4,128)}, f32[3,2048]{1,0:T(4,128)S(1)}, u32[]{:S(2)}) copy-start(f32[3,2048]{1,0:T(4,128)S(1)} %get-tuple-element.375) | copy-start | bytes 73732
  38.3 20.1 %copy-start.30 = (f32[3,2048]{1,0:T(4,128)}, f32[3,2048]{1,0:T(4,128)S(1)}, u32[]{:S(2)}) copy-start(f32[3,2048]{1,0:T(4,128)S(1)} %get-tuple-element.376) | copy-start | bytes 73732
  364.8 4.7 copy-start.10
  386.4 24.1 %copy-start.9 = (f32[16,2048]{1,0:T(8,128)S(1)}, f32[16,2048]{1,0:T(8,128)}, u32[]{:S(2)}) copy-start(f32[16,2048]{1,0:T(8,128)} %custom-call.1) | copy-start | bytes 393220
  410.5 8.6 %copy-start.35 = (f32[8]{0:T(128)S(1)}, f32[8]{0:T(128)}, u32[]{:S(2)}) copy-start(f32[8]{0:T(128)} %subtract_multiply_fusion) | copy-start | bytes 100
  513.2 7.6 %copy-start.11 = (f32[16,2048]{1,0:T(8,128)S(1)}, f32[16,2048]{1,0:T(8,128)}, u32[]{:S(2)}) copy-start(f32[16,2048]{1,0:T(8,128)} %get-tuple-element.365) | copy-start | bytes 393220
  519.3 4.8 copy-start.17
  534.6 29.7 %copy-start.8 = (f32[16,2048]{1,0:T(8,128)S(1)}, f32[16,2048]{1,0:T(8,128)}, u32[]{:S(2)}) copy-start(f32[16,2048]{1,0:T(8,128)} %custom-call) | copy-start | bytes 393220
  544.7 25.1 %copy-start.34 = (f32[8]{0:T(128)S(1)}, f32[8]{0:T(128)}, u32[]{:S(2)}) copy-start(f32[8]{0:T(128)} %iota_multiply_fusion) | copy-start | bytes 100
  646.3 2.5 copy-start.4
  646.3 7.8 %slice-start = ((s8[16777216]{0:T(1024)(128)(4,1)}), s8[4194304]{0:T(1024)(128)(4,1)S(1)}, s32[]{:S(2)}) async-start(s8[16777216]{0:T(1024)(128)(4,1)} %bitcast.94), calls=%async_computation.4 | async-start | bytes 8388608
  648.6 4.0 copy-start.6
  648.8 5.3 slice-start.1
  648.8 5.3 slice-start.2
  648.8 5.9 slice-start.3
  658.0 41.2 %copy-start.3 = (f32[1,128,2048]{2,1,0:T(8,128)S(1)}, f32[1,128,2048]{2,1,0:T(8,128)}, u32[]{:S(2)}) copy-start(f32[1,128,2048]{2,1,0:T(8,128)} %get-tuple-element.334) | copy-start | bytes 3145732
  658.0 41.2 %copy-start.5 = (f32[1,128,2048]{2,1,0:T(8,128)S(1)}, f32[1,128,2048]{2,1,0:T(8,128)}, u32[]{:S(2)}) copy-start(f32[1,128,2048]{2,1,0:T(8,128)} %get-tuple-element.335) | copy-start | bytes 3145732
  658.0 41.2 %copy-start.7 = (f32[128,2048]{1,0:T(8,128)S(1)}, f32[128,2048]{1,0:T(8,128)}, u32[]{:S(2)}) copy-start(f32[128,2048]{1,0:T(8,128)} %copy-done.6) | copy-start | bytes 3145732
  679.1 20.1 %collective-permute-start.1 = (bf16[3,6,2048]{2,1,0:T(8,128)(2,1)S(1)}, bf16[3,6,2048]{2,1,0:T(8,128)(2,1)S(1)}, u32[]{:S(2)}, u32[]{:S(2)}) collective-permute-start(bf16[3,6,2048]{2,1,0:T(8,128)(2,1)S(1)} %slice.494), channel_id=1, source_target_pairs={{4,0},{8,4},{12,8},{5,1},{9,5},{13,9},{6,2},{10,6},{14,10},{7,3},{... | collective-permute-start | bytes 221192 | tf_op jit(solution)/shard_map/ppermute | solution.py:12
  (13 other events, 14.2 us)
Sparse Core Ops, SparseCore 0:
  9.6 19.4 all-gather.5
  30.6 288.7 all-gather.3
  658.1 23.9 reduce-scatter.1
where the time goes:
time: 718 us; the launch traced here: 711 us
  waiting for transfers between devices  258 us (36%)
  matrix products  169 us (24%)
  local copies, waits for them, and re-layouts  131 us (18%)
  blocking collectives  65.8 us (9%)
  other arithmetic  64.7 us (9%)
  between operations  14.6 us (2%)
    all_gather x1, waiting for transfers between devices, shards(): weights = lax.all_gather(out_weight, 'ctx', axis=1, tiled=True)  257 us
    all_gather x3, blocking collectives, entering(): lax.all_gather(part.astype(kind), axis)  47.7 us
    dot_general x1, matrix products, shards(): jnp.einsum('tsc,bsc->btc', toeplitz, gated_blocks, precision=highest)  32 us
    dot_general x1, matrix products, shards(): jnp.einsum('snc,bnc->bsc', tail_powers, exit_adjoint, precision=highest)  30.3 us
    dot_general x1, matrix products, shards(): jnp.einsum('tnc,bnc->btc', lead_powers, entry_states, precision=highest)  30.3 us
    unnamed x93, local copies, waits for them, and re-layouts  20.2 us
    dot_general x1, matrix products, shards(): jnp.einsum('tsc,btc->bsc', toeplitz, grad_mixed, precision=highest)  20 us
    dot_general x1, matrix products, shards(): jnp.einsum('snc,bsc->bnc', end_powers, gated_blocks, precision=highest)  19.7 us
  transfers between devices with their start and end apart: 5, of which 1 were waited for; matrix products, arithmetic and copies ran while one was open for 8% of the time, Pallas kernels for 0%

commit v1 on v0

--- a/solution.py
+++ b/solution.py
@@ -1,6 +1,10 @@
+import functools
+
 import jax
 import jax.numpy as jnp
 from jax import lax
+from jax.experimental import pallas as pl
+from jax.experimental.pallas import tpu as pltpu
 from jax.sharding import PartitionSpec as P
 
 block_rows = 16
@@ -139,6 +143,569 @@
     return (output, input_grads[0], input_grads[1], input_grads[2], grad_short)
 
 
+LANES = 128
+MESH = pl.DeviceIdType.MESH
+
+
+def remote(src, dst, send, recv, where):
+    return pltpu.make_async_remote_copy(
+        src_ref=src, dst_ref=dst, send_sem=send, recv_sem=recv, device_id=where, device_id_type=MESH
+    )
+
+
+def fused_kernel(
+    n,
+    q_ref,
+    k_ref,
+    v_ref,
+    taps_ref,
+    rates_ref,
+    scaled_ref,
+    w_ref,
+    cot_ref,
+    out_ref,
+    gq_ref,
+    gk_ref,
+    gv_ref,
+    gs_ref,
+    halo,
+    xp,
+    conv,
+    seq_in,
+    seq_out,
+    end_mine,
+    end_in,
+    entry,
+    cot_all,
+    part,
+    part_in,
+    prod_all,
+    opart,
+    opart_in,
+    osum,
+    ofin,
+    ge,
+    ghalo_mine,
+    ghalo,
+    fsum,
+    fs_mine,
+    fs_in,
+    cot_sem,
+    cot_send,
+    cot_recv,
+    halo_send,
+    halo_recv,
+    state_send,
+    state_recv,
+    adj_send,
+    adj_recv,
+    rs_send,
+    rs_recv,
+    ag_send,
+    ag_recv,
+    ors_send,
+    ors_recv,
+    fin_sem,
+    gh_send,
+    gh_recv,
+    fs_send,
+    fs_recv,
+):
+    c = lax.axis_index("ctx")
+    p = lax.axis_index("tp")
+    L, C = q_ref.shape
+    N = w_ref.shape[1]
+    taps = taps_ref.shape[1]
+    ncb = C // LANES
+    modes = rates_ref.shape[0] // ncb
+    halves = ncb // 8
+    inputs = (q_ref, k_ref, v_ref)
+
+    def ctx_at(d):
+        return lax.rem(c + d + n, n)
+
+    def tp_at(d):
+        return lax.rem(p + d + n, n)
+
+    def rows_of(i):
+        return pl.ds(pl.multiple_of(i * L, L), L)
+
+    def cols_of(i, width=LANES):
+        return pl.ds(pl.multiple_of(i * width, width), width)
+
+    barrier = pltpu.get_barrier_semaphore()
+    for d in range(1, n):
+        pl.semaphore_signal(barrier, inc=1, device_id={"ctx": ctx_at(d)}, device_id_type=MESH)
+        pl.semaphore_signal(barrier, inc=1, device_id={"tp": tp_at(d)}, device_id_type=MESH)
+
+    @pl.when(c != p)
+    def _():
+        pl.semaphore_signal(barrier, inc=1, device_id={"ctx": p, "tp": c}, device_id_type=MESH)
+
+    @pl.when(c != p)
+    def _():
+        pl.semaphore_wait(barrier, 2 * (n - 1) + 1)
+
+    @pl.when(c == p)
+    def _():
+        pl.semaphore_wait(barrier, 2 * (n - 1))
+
+    halo_copies = [
+        remote(
+            x.at[pl.ds(L - 16, 16), :],
+            halo.at[b],
+            halo_send.at[b],
+            halo_recv.at[b],
+            {"ctx": ctx_at(1)},
+        )
+        for b, x in enumerate(inputs)
+    ]
+
+    @pl.when(c < n - 1)
+    def _():
+        for copy in halo_copies:
+            copy.start()
+
+    cot_turn = remote(
+        cot_ref, cot_all.at[rows_of(c), :], cot_sem.at[0], cot_sem.at[1], {"ctx": p, "tp": c}
+    )
+    cot_keep = pltpu.make_async_copy(cot_ref, cot_all.at[rows_of(c), :], cot_sem.at[2])
+
+    @pl.when(c != p)
+    def _():
+        cot_turn.start()
+
+    @pl.when(c == p)
+    def _():
+        cot_keep.start()
+
+    @pl.when(c == 0)
+    def _():
+        halo[...] = jnp.zeros(halo.shape, halo.dtype)
+
+    @pl.when(c > 0)
+    def _():
+        for copy in halo_copies:
+            copy.wait_recv()
+
+    def conv_block(i, carry):
+        col = cols_of(i)
+        done = []
+        for b, x in enumerate(inputs):
+            at = b * ncb + i
+            xp[at, 0:8, :] = halo[b, :, col].astype(jnp.float32)[8:16]
+            xp[at, 8 : 8 + L, :] = x[:, col].astype(jnp.float32)
+            acc = taps_ref[b, 0:1, col] * xp[at, 8 : 8 + L, :]
+            for j in range(1, taps):
+                acc = acc + taps_ref[b, j : j + 1, col] * xp[at, 8 - j : 8 - j + L, :]
+            conv[at] = acc
+            done.append(acc)
+        seq_in[pl.ds(i, L, stride=ncb), :] = done[1] * done[2]
+        return carry
+
+    half_blocks = ncb // 2
+    lax.fori_loop(0, half_blocks, conv_block, 0)
+
+    @pl.when(c != p)
+    def _():
+        cot_turn.wait_recv()
+
+    @pl.when(c == p)
+    def _():
+        cot_keep.wait()
+
+    cot_copies = [
+        remote(
+            cot_all.at[rows_of(p), :],
+            cot_all.at[rows_of(p), :],
+            cot_send.at[d - 1],
+            cot_recv.at[d - 1],
+            {"tp": tp_at(d)},
+        )
+        for d in range(1, n)
+    ]
+    for copy in cot_copies:
+        copy.start()
+
+    lax.fori_loop(half_blocks, ncb, conv_block, 0)
+
+    def mode_rows(k, h):
+        return pl.ds(k * ncb + h * 8, 8)
+
+    def last_state(reverse):
+        for h in range(halves):
+            lam = [jnp.exp(-rates_ref[mode_rows(k, h), :]) for k in range(modes)]
+
+            def step(t, states):
+                for u in range(4):
+                    at = 4 * t + u
+                    if reverse:
+                        at = L - 1 - at
+                    x = seq_in[pl.ds(pl.multiple_of(at * ncb + h * 8, 8), 8), :]
+                    states = tuple(a * s + x for a, s in zip(lam, states))
+                return states
+
+            zero = jnp.zeros((8, LANES), jnp.float32)
+            states = lax.fori_loop(0, L // 4, step, (zero,) * modes)
+            for k in range(modes):
+                entry[mode_rows(k, h), :] = states[k]
+        end_mine[...] = entry[...].astype(jnp.bfloat16)
+
+    def state_copies(sign, send, recv, slot):
+        return [
+            remote(
+                end_mine,
+                end_in.at[slot, d - 1],
+                send.at[d - 1],
+                recv.at[d - 1],
+                {"ctx": ctx_at(sign * d)},
+            )
+            for d in range(1, n)
+        ]
+
+    def enter(slot, position):
+        total = jnp.zeros(entry.shape, jnp.float32)
+        for d in range(1, n):
+            term = end_in[slot, d - 1].astype(jnp.float32)
+            if d > 1:
+                term = term * jnp.exp(-rates_ref[...] * float(L * (d - 1)))
+            total = total + jnp.where(position >= d, term, 0.0)
+        entry[...] = total
+
+    def run(reverse):
+        for h in range(halves):
+            lam = [jnp.exp(-rates_ref[mode_rows(k, h), :]) for k in range(modes)]
+            gain = [scaled_ref[mode_rows(k, h), :] for k in range(modes)]
+
+            def step(t, states):
+                for u in range(2):
+                    at = 2 * t + u
+                    if reverse:
+                        at = L - 1 - at
+                    here = pl.ds(pl.multiple_of(at * ncb + h * 8, 8), 8)
+                    x = seq_in[here, :]
+                    states = tuple(a * s + x for a, s in zip(lam, states))
+                    terms = [g * s for g, s in zip(gain, states)]
+                    sums = [terms[m] for m in range(4)]
+                    for m in range(4, modes):
+                        sums[m % 4] = sums[m % 4] + terms[m]
+                    seq_out[here, :] = (sums[0] + sums[1]) + (sums[2] + sums[3])
+                return states
+
+            first = tuple(entry[mode_rows(k, h), :] for k in range(modes))
+            lax.fori_loop(0, L // 2, step, first)
+
+    last_state(False)
+    forward_states = state_copies(1, state_send, state_recv, 0)
+    for copy in forward_states:
+        copy.start()
+
+    for copy in cot_copies:
+        copy.wait_recv()
+
+    tile = min(256, C)
+
+    def grad_tile(i, carry):
+        col = cols_of(i, tile)
+        value = lax.dot_general(
+            cot_all[...],
+            w_ref[col, :],
+            (((1,), (1,)), ((), ())),
+            preferred_element_type=jnp.float32,
+        )
+        part[:, col] = value.astype(jnp.bfloat16)
+        return carry
+
+    lax.fori_loop(0, C // tile, grad_tile, 0)
+    rs_copies = [
+        remote(
+            part.at[rows_of(ctx_at(d)), :],
+            part_in.at[d - 1],
+            rs_send.at[d - 1],
+            rs_recv.at[d - 1],
+            {"ctx": ctx_at(d)},
+        )
+        for d in range(1, n)
+    ]
+    for copy in rs_copies:
+        copy.start()
+
+    for copy in forward_states:
+        copy.wait_recv()
+    enter(0, c)
+    run(False)
+
+    def product_block(i, carry):
+        mixed = seq_out[pl.ds(i, L, stride=ncb), :]
+        prod_all[rows_of(c), cols_of(i)] = (conv[i] * mixed).astype(jnp.bfloat16)
+        return carry
+
+    lax.fori_loop(0, ncb, product_block, 0)
+    ag_copies = [
+        remote(
+            prod_all.at[rows_of(c), :],
+            prod_all.at[rows_of(c), :],
+            ag_send.at[d - 1],
+            ag_recv.at[d - 1],
+            {"ctx": ctx_at(d)},
+        )
+        for d in range(1, n)
+    ]
+    for copy in ag_copies:
+        copy.start()
+
+    for copy in forward_states:
+        copy.wait_send()
+    for copy in rs_copies:
+        copy.wait_recv()
+
+    def grad_block(i, carry):
+        col = cols_of(i)
+        grad = part[rows_of(c), col].astype(jnp.float32)
+        for d in range(1, n):
+            grad = grad + part_in[d - 1, :, col].astype(jnp.float32)
+        mixed = seq_out[pl.ds(i, L, stride=ncb), :]
+        ge[i, 0:L, :] = grad * mixed
+        ghalo_mine[0, :, col] = (grad * mixed)[0:16].astype(jnp.bfloat16)
+        seq_in[pl.ds(i, L, stride=ncb), :] = grad * conv[i]
+        return carry
+
+    lax.fori_loop(0, ncb, grad_block, 0)
+    last_state(True)
+    backward_states = state_copies(-1, adj_send, adj_recv, 1)
+    for copy in backward_states:
+        copy.start()
+
+    for copy in ag_copies:
+        copy.wait_recv()
+    otile = min(256, N)
+
+    def out_tile(i, carry):
+        col = cols_of(i, otile)
+        value = jnp.dot(prod_all[...], w_ref[:, col], preferred_element_type=jnp.float32)
+        opart[:, col] = value.astype(jnp.bfloat16)
+        return carry
+
+    lax.fori_loop(0, N // otile, out_tile, 0)
+    ors_copies = [
+        remote(
+            opart.at[rows_of(tp_at(d)), :],
+            opart_in.at[d - 1],
+            ors_send.at[d - 1],
+            ors_recv.at[d - 1],
+            {"tp": tp_at(d)},
+        )
+        for d in range(1, n)
+    ]
+    for copy in ors_copies:
+        copy.start()
+
+    for copy in backward_states:
+        copy.wait_recv()
+    enter(1, n - 1 - c)
+    run(True)
+
+    def gated_block(i, carry):
+        col = cols_of(i)
+        grad = seq_out[pl.ds(i, L, stride=ncb), :]
+        for b, other in ((1, 2), (2, 1)):
+            value = grad * conv[other * ncb + i]
+            ge[b * ncb + i, 0:L, :] = value
+            ghalo_mine[b, :, col] = value[0:16].astype(jnp.bfloat16)
+        return carry
+
+    lax.fori_loop(0, ncb, gated_block, 0)
+    gh_copy = remote(ghalo_mine, ghalo, gh_send, gh_recv, {"ctx": ctx_at(-1)})
+
+    @pl.when(c > 0)
+    def _():
+        gh_copy.start()
+
+    for copy in ors_copies:
+        copy.wait_recv()
+    total = opart[rows_of(p), :].astype(jnp.float32)
+    for d in range(1, n):
+        total = total + opart_in[d - 1].astype(jnp.float32)
+    osum[...] = total.astype(jnp.bfloat16)
+    fin_turn = remote(osum, ofin, fin_sem.at[0], fin_sem.at[1], {"ctx": p, "tp": c})
+
+    @pl.when(c != p)
+    def _():
+        fin_turn.start()
+
+    fsum[...] = jnp.zeros(fsum.shape, fsum.dtype)
+    group = C // fsum.shape[1]
+
+    def filter_block(i, carry):
+        lane = lax.broadcasted_iota(jnp.int32, (LANES, fsum.shape[1]), 0) + i * LANES
+        low = lax.broadcasted_iota(jnp.int32, (LANES, fsum.shape[1]), 1) * group
+        member = jnp.where((lane >= low) & (lane < low + group), 1.0, 0.0)
+        for b in range(3):
+            at = b * ncb + i
+            grad = ge[at, 0:L, :]
+            for j in range(taps):
+                fs_mine[b * 8 + j : b * 8 + j + 1, :] = jnp.sum(
+                    grad * xp[at, 8 - j : 8 - j + L, :], axis=0, keepdims=True
+                )
+        fsum[...] += jnp.dot(
+            fs_mine[...],
+            member,
+            precision=lax.Precision.HIGHEST,
+            preferred_element_type=jnp.float32,
+        )
+        return carry
+
+    fs_mine[...] = jnp.zeros(fs_mine.shape, fs_mine.dtype)
+    lax.fori_loop(0, ncb, filter_block, 0)
+    fs_copies = [
+        remote(
+            fsum, fs_in.at[d - 1], fs_send.at[d - 1], fs_recv.at[d - 1], {"ctx": ctx_at(d)}
+        )
+        for d in range(1, n)
+    ]
+    for copy in fs_copies:
+        copy.start()
+
+    @pl.when(c == n - 1)
+    def _():
+        ghalo[...] = jnp.zeros(ghalo.shape, ghalo.dtype)
+
+    @pl.when(c < n - 1)
+    def _():
+        gh_copy.wait_recv()
+
+    def input_block(i, carry):
+        col = cols_of(i)
+        for b, g_ref in enumerate((gq_ref, gk_ref, gv_ref)):
+            at = b * ncb + i
+            ge[at, L : L + 8, :] = ghalo[b, :, col].astype(jnp.float32)[0:8]
+            acc = taps_ref[b, 0:1, col] * ge[at, 0:L, :]
+            for j in range(1, taps):
+                acc = acc + taps_ref[b, j : j + 1, col] * ge[at, j : j + L, :]
+            g_ref[:, col] = acc.astype(jnp.bfloat16)
+        return carry
+
+    lax.fori_loop(0, ncb, input_block, 0)
+
+    for copy in fs_copies:
+        copy.wait_recv()
+    sums = fsum[...]
+    for d in range(1, n):
+        sums = sums + fs_in[d - 1]
+    gs_ref[...] = sums / float(L * n)
+
+    @pl.when(c != p)
+    def _():
+        fin_turn.wait_recv()
+        out_ref[...] = ofin[...]
+
+    @pl.when(c == p)
+    def _():
+        out_ref[...] = osum[...]
+
+    @pl.when(c != p)
+    def _():
+        cot_turn.wait_send()
+        fin_turn.wait_send()
+
+    @pl.when(c < n - 1)
+    def _():
+        for copy in halo_copies:
+            copy.wait_send()
+
+    @pl.when(c > 0)
+    def _():
+        gh_copy.wait_send()
+
+    for copy in cot_copies + rs_copies + ag_copies + backward_states + ors_copies + fs_copies:
+        copy.wait_send()
+
+
+def fused_shards(n, q_in, k_in, v_in, short_filters, rates, residues, out_weight, cotangent):
+    L, C = q_in.shape
+    N = out_weight.shape[1]
+    modes = rates.shape[0]
+    groups, taps = short_filters.shape[1:]
+    ncb = C // LANES
+    rows = modes * ncb
+    filter_rows = jnp.repeat(jnp.transpose(short_filters, (0, 2, 1)), C // groups, axis=2)
+    scaled = residues * jnp.sqrt(-jnp.expm1(-2.0 * rates))
+    bf16, f32 = jnp.bfloat16, jnp.float32
+    dma = pltpu.SemaphoreType.DMA
+    vmem = pl.BlockSpec(memory_space=pltpu.VMEM)
+    m = n - 1
+    outs = pl.pallas_call(
+        functools.partial(fused_kernel, n),
+        out_shape=(
+            jax.ShapeDtypeStruct((L, N), bf16),
+            jax.ShapeDtypeStruct((L, C), bf16),
+            jax.ShapeDtypeStruct((L, C), bf16),
+            jax.ShapeDtypeStruct((L, C), bf16),
+            jax.ShapeDtypeStruct((24, groups), f32),
+        ),
+        in_specs=[vmem] * 8,
+        out_specs=(vmem,) * 5,
+        scratch_shapes=[
+            pltpu.VMEM((3, 16, C), bf16),
+            pltpu.VMEM((3 * ncb, L + 8, LANES), f32),
+            pltpu.VMEM((3 * ncb, L, LANES), f32),
+            pltpu.VMEM((L * ncb, LANES), f32),
+            pltpu.VMEM((L * ncb, LANES), f32),
+            pltpu.VMEM((rows, LANES), bf16),
+            pltpu.VMEM((2, m, rows, LANES), bf16),
+            pltpu.VMEM((rows, LANES), f32),
+            pltpu.VMEM((n * L, N), bf16),
+            pltpu.VMEM((n * L, C), bf16),
+            pltpu.VMEM((m, L, C), bf16),
+            pltpu.VMEM((n * L, C), bf16),
+            pltpu.VMEM((n * L, N), bf16),
+            pltpu.VMEM((m, L, N), bf16),
+            pltpu.VMEM((L, N), bf16),
+            pltpu.VMEM((L, N), bf16),
+            pltpu.VMEM((3 * ncb, L + 8, LANES), f32),
+            pltpu.VMEM((3, 16, C), bf16),
+            pltpu.VMEM((3, 16, C), bf16),
+            pltpu.VMEM((24, groups), f32),
+            pltpu.VMEM((24, LANES), f32),
+            pltpu.VMEM((m, 24, groups), f32),
+            dma((3,)),
+            dma((m,)),
+            dma((m,)),
+            dma((3,)),
+            dma((3,)),
+            dma((m,)),
+            dma((m,)),
+            dma((m,)),
+            dma((m,)),
+            dma((m,)),
+            dma((m,)),
+            dma((m,)),
+            dma((m,)),
+            dma((m,)),
+            dma((m,)),
+            dma((2,)),
+            dma,
+            dma,
+            dma((m,)),
+            dma((m,)),
+        ],
+        compiler_params=pltpu.CompilerParams(
+            collective_id=0, has_side_effects=True, vmem_limit_bytes=56 * 1024 * 1024
+        ),
+    )(
+        q_in,
+        k_in,
+        v_in,
+        filter_rows,
+        rates.reshape(rows, LANES),
+        scaled.reshape(rows, LANES),
+        out_weight,
+        cotangent,
+    )
+    grad_short = jnp.transpose(outs[4].reshape(3, 8, groups)[:, :taps], (0, 2, 1))
+    return outs[:4] + (grad_short,)
+
+
 def solution(mesh):
     placed = (
         P(("groups", "ctx"), "tp"),
@@ -150,8 +717,12 @@
         P("tp", "ctx"),
         P(("groups", "ctx"), "tp"),
     )
+    n = mesh.shape["ctx"]
+    body = shards
+    if n == mesh.shape["tp"] == 4:
+        body = functools.partial(fused_shards, n)
     return jax.shard_map(
-        shards,
+        body,
         mesh=mesh,
         in_specs=placed,
         out_specs=(

time: 718 us -> 172 us (0.24)
  the two profiles are of different devices: /device:TPU:0 before, /device:TPU:1 now
where the time goes in v1:
time: 172 us; the launch traced here: 171 us
  Pallas kernels  156 us (91%)
  local copies, waits for them, and re-layouts  13.5 us (8%)
    pallas_call x1, Pallas kernels, fused_shards(): pl.pallas_call(functools.partial(fused_kernel, n), out_shape=(jax.ShapeDt...  156 us
    unnamed x4, local copies, waits for them, and re-layouts  7.31 us

profile of v1, /device:TPU:1, one launch (start us, length us, event | category | flops | bytes accessed | tf_op | source)
XLA Modules:
  0.0 171.1 jit_solution(8847460373432593676)
XLA Ops:
  0.6 1.1 sqrt_multiply_fusion
  1.7 0.7 reshape.24.scaled_ref
  2.4 1.6 reshape.23.rates_ref
  4.0 1.1 broadcast_in_dim.3
  5.1 1.5 reshape.22.taps_ref
  6.5 155.9 %shard_map.119 = (bf16[128,1024]{1,0:T(8,128)(2,1)}, bf16[128,2048]{1,0:T(8,128)(2,1)}, bf16[128,2048]{1,0:T(8,128)(2,1)}, bf16[128,2048]{1,0:T(8,128)(2,1)}, f32[24,128]{1,0:T(8,128)}) custom-call(bf16[128,2048]{1,0:T(8,128)(2,1)} %q_ref.1, bf16[128,2048]{1,0:T(8,128)(2,1)} %k_ref.1, bf16[128,2048]{1,0:T(8,128)(2,1)} %v_ref.1, ...), custom_call_target="tpu_custom_call" | custom-call | tf_op jit(solution)/shard_map/pallas_call | solution.py:637
  162.5 1.3 slice_bitcast_fusion
  163.8 1.7 copy.17
  165.4 1.9 %copy.18 = bf16[128,2048]{1,0:T(8,128)(2,1)} copy(bf16[128,2048]{1,0:T(8,128)(2,1)} %get-tuple-element.21) | data formatting | bytes 1048576
  167.3 1.9 %copy.19 = bf16[128,2048]{1,0:T(8,128)(2,1)} copy(bf16[128,2048]{1,0:T(8,128)(2,1)} %get-tuple-element.22) | data formatting | bytes 1048576
  169.2 1.9 %copy.20 = bf16[128,2048]{1,0:T(8,128)(2,1)} copy(bf16[128,2048]{1,0:T(8,128)(2,1)} %get-tuple-element.23) | data formatting | bytes 1048576

commit v2 on v1

--- a/solution.py
+++ b/solution.py
@@ -219,6 +219,7 @@
     ncb = C // LANES
     modes = rates_ref.shape[0] // ncb
     halves = ncb // 8
+    m = n - 1
     inputs = (q_ref, k_ref, v_ref)
 
     def ctx_at(d):
@@ -386,9 +387,9 @@
                     x = seq_in[here, :]
                     states = tuple(a * s + x for a, s in zip(lam, states))
                     terms = [g * s for g, s in zip(gain, states)]
-                    sums = [terms[m] for m in range(4)]
-                    for m in range(4, modes):
-                        sums[m % 4] = sums[m % 4] + terms[m]
+                    sums = terms[:4]
+                    for k in range(4, modes):
+                        sums[k % 4] = sums[k % 4] + terms[k]
                     seq_out[here, :] = (sums[0] + sums[1]) + (sums[2] + sums[3])
                 return states
 
@@ -417,18 +418,93 @@
         return carry
 
     lax.fori_loop(0, C // tile, grad_tile, 0)
-    rs_copies = [
-        remote(
-            part.at[rows_of(ctx_at(d)), :],
-            part_in.at[d - 1],
-            rs_send.at[d - 1],
-            rs_recv.at[d - 1],
-            {"ctx": ctx_at(d)},
-        )
-        for d in range(1, n)
-    ]
-    for copy in rs_copies:
-        copy.start()
+
+    def place(way):
+        return c if way == 0 else n - 1 - c
+
+    def rs_chunk(way, at):
+        return at if way == 0 else n - 1 - at
+
+    def rs_copy(way, s):
+        return remote(
+            part.at[rows_of(rs_chunk(way, n - 1 - s + place(way))), :],
+            part_in.at[way * m + s],
+            rs_send.at[way * m + s],
+            rs_recv.at[way * m + s],
+            {"ctx": ctx_at(1 - 2 * way)},
+        )
+
+    def rs_sends(way, s):
+        return (place(way) < n - 1) & (place(way) <= s)
+
+    def rs_start(s):
+        for way in range(2):
+
+            @pl.when(rs_sends(way, s))
+            def _():
+                rs_copy(way, s).start()
+
+    def rs_arrive(s):
+        for way in range(2):
+
+            @pl.when((place(way) > 0) & (place(way) <= s + 1))
+            def _():
+                pltpu.make_async_remote_copy(
+                    src_ref=part_in.at[way * m + s],
+                    dst_ref=part_in.at[way * m + s],
+                    send_sem=rs_send.at[way * m + s],
+                    recv_sem=rs_recv.at[way * m + s],
+                    device_id={"ctx": ctx_at(1 - 2 * way)},
+                    device_id_type=MESH,
+                ).wait_recv()
+                if s < m - 1:
+                    mine = rows_of(rs_chunk(way, n - 2 - s + place(way)))
+
+                    def add_block(i, carry):
+                        col = cols_of(i)
+                        value = part[mine, col].astype(jnp.float32)
+                        value = value + part_in[way * m + s, :, col].astype(jnp.float32)
+                        part[mine, col] = value.astype(jnp.bfloat16)
+                        return carry
+
+                    lax.fori_loop(0, ncb, add_block, 0)
+
+    def ag_copy(way, s, back):
+        rows = rows_of(c - (1 - 2 * way) * (s + back))
+        return remote(
+            prod_all.at[rows, :],
+            prod_all.at[rows, :],
+            ag_send.at[way * m + s],
+            ag_recv.at[way * m + s],
+            {"ctx": ctx_at(1 - 2 * way)},
+        )
+
+    def ag_sends(way, s):
+        return (place(way) < n - 1) & (place(way) >= s)
+
+    def ag_start(s):
+        for way in range(2):
+
+            @pl.when(ag_sends(way, s))
+            def _():
+                ag_copy(way, s, 0).start()
+
+    def ag_arrive(s):
+        for way in range(2):
+
+            @pl.when(place(way) > s)
+            def _():
+                ag_copy(way, s, 1).wait_recv()
+
+    @pl.when(c == 0)
+    def _():
+        part_in[m - 1] = jnp.zeros((L, C), jnp.bfloat16)
+
+    @pl.when(c == n - 1)
+    def _():
+        part_in[2 * m - 1] = jnp.zeros((L, C), jnp.bfloat16)
+
+    rs_start(0)
 
     for copy in forward_states:
         copy.wait_recv()
@@ -441,29 +517,21 @@
         return carry
 
     lax.fori_loop(0, ncb, product_block, 0)
-    ag_copies = [
-        remote(
-            prod_all.at[rows_of(c), :],
-            prod_all.at[rows_of(c), :],
-            ag_send.at[d - 1],
-            ag_recv.at[d - 1],
-            {"ctx": ctx_at(d)},
-        )
-        for d in range(1, n)
-    ]
-    for copy in ag_copies:
-        copy.start()
-
+    ag_start(0)
     for copy in forward_states:
         copy.wait_send()
-    for copy in rs_copies:
-        copy.wait_recv()
+    for hop in range(1, m):
+        rs_arrive(hop - 1)
+        rs_start(hop)
+        ag_arrive(hop - 1)
+        ag_start(hop)
+    rs_arrive(m - 1)
 
     def grad_block(i, carry):
         col = cols_of(i)
         grad = part[rows_of(c), col].astype(jnp.float32)
-        for d in range(1, n):
-            grad = grad + part_in[d - 1, :, col].astype(jnp.float32)
+        for way in range(2):
+            grad = grad + part_in[way * m + m - 1, :, col].astype(jnp.float32)
         mixed = seq_out[pl.ds(i, L, stride=ncb), :]
         ge[i, 0:L, :] = grad * mixed
         ghalo_mine[0, :, col] = (grad * mixed)[0:16].astype(jnp.bfloat16)
@@ -476,8 +544,7 @@
     for copy in backward_states:
         copy.start()
 
-    for copy in ag_copies:
-        copy.wait_recv()
+    ag_arrive(m - 1)
     otile = min(256, N)
 
     def out_tile(i, carry):
@@ -617,7 +684,18 @@
     def _():
         gh_copy.wait_send()
 
-    for copy in cot_copies + rs_copies + ag_copies + backward_states + ors_copies + fs_copies:
+    for hop in range(m):
+        for way in range(2):
+
+            @pl.when(rs_sends(way, hop))
+            def _():
+                rs_copy(way, hop).wait_send()
+
+            @pl.when(ag_sends(way, hop))
+            def _():
+                ag_copy(way, hop, 0).wait_send()
+
+    for copy in cot_copies + backward_states + ors_copies + fs_copies:
         copy.wait_send()
 
 
@@ -656,7 +734,7 @@
             pltpu.VMEM((rows, LANES), f32),
             pltpu.VMEM((n * L, N), bf16),
             pltpu.VMEM((n * L, C), bf16),
-            pltpu.VMEM((m, L, C), bf16),
+            pltpu.VMEM((2 * m, L, C), bf16),
             pltpu.VMEM((n * L, C), bf16),
             pltpu.VMEM((n * L, N), bf16),
             pltpu.VMEM((m, L, N), bf16),
@@ -677,10 +755,10 @@
             dma((m,)),
             dma((m,)),
             dma((m,)),
-            dma((m,)),
-            dma((m,)),
-            dma((m,)),
-            dma((m,)),
+            dma((2 * m,)),
+            dma((2 * m,)),
+            dma((2 * m,)),
+            dma((2 * m,)),
             dma((m,)),
             dma((m,)),
             dma((2,)),

time: 172 us -> 141 us (0.82)
  Pallas kernels: 156 us -> 126 us
    pallas_call x1, Pallas kernels: 156 us -> 126 us  [fused_shards(): pl.pallas_call(functools.partial(fused_kernel, n), out_shape=(jax.ShapeDt...]
where the time goes in v2:
time: 141 us
  Pallas kernels  126 us (89%)
  local copies, waits for them, and re-layouts  13.5 us (10%)
    pallas_call x1, Pallas kernels, fused_shards(): pl.pallas_call(functools.partial(fused_kernel, n), out_shape=(jax.ShapeDt...  126 us
    unnamed x4, local copies, waits for them, and re-layouts  7.31 us

profile of v2, /device:TPU:1, one launch (start us, length us, event | category | flops | bytes accessed | tf_op | source)
XLA Modules:
  0.0 140.7 jit_solution(14904262997568156639)
XLA Ops:
  0.6 1.1 sqrt_multiply_fusion
  1.7 0.7 reshape.24.scaled_ref
  2.4 1.6 %reshape.23.rates_ref = f32[256,128]{1,0:T(8,128)} reshape(f32[16,2048]{1,0:T(8,128)} %param.12) | data formatting | bytes 262144 | tf_op jit(solution)/shard_map/reshape | solution.py:778
  4.0 1.1 broadcast_in_dim.3
  5.1 1.5 %reshape.22.taps_ref = f32[3,7,2048]{2,1,0:T(8,128)} reshape(f32[3,7,128,16]{3,2,1,0:T(8,128)S(1)} %broadcast_in_dim.3) | data formatting | bytes 344064 | tf_op jit(solution)/shard_map/reshape | solution.py:709
  6.5 125.6 %shard_map.119 = (bf16[128,1024]{1,0:T(8,128)(2,1)}, bf16[128,2048]{1,0:T(8,128)(2,1)}, bf16[128,2048]{1,0:T(8,128)(2,1)}, bf16[128,2048]{1,0:T(8,128)(2,1)}, f32[24,128]{1,0:T(8,128)}) custom-call(bf16[128,2048]{1,0:T(8,128)(2,1)} %q_ref.1, bf16[128,2048]{1,0:T(8,128)(2,1)} %k_ref.1, bf16[128,2048]{1,0:T(8,128)(2,1)} %v_ref.1, ...), custom_call_target="tpu_custom_call" | custom-call | tf_op jit(solution)/shard_map/pallas_call | solution.py:715
  132.1 1.3 slice_bitcast_fusion
  133.4 1.7 %copy.17 = bf16[128,1024]{1,0:T(8,128)(2,1)} copy(bf16[128,1024]{1,0:T(8,128)(2,1)} %get-tuple-element.20) | data formatting | bytes 524288
  135.1 1.9 %copy.18 = bf16[128,2048]{1,0:T(8,128)(2,1)} copy(bf16[128,2048]{1,0:T(8,128)(2,1)} %get-tuple-element.21) | data formatting | bytes 1048576
  137.0 1.9 %copy.19 = bf16[128,2048]{1,0:T(8,128)(2,1)} copy(bf16[128,2048]{1,0:T(8,128)(2,1)} %get-tuple-element.22) | data formatting | bytes 1048576
  138.8 1.9 %copy.20 = bf16[128,2048]{1,0:T(8,128)(2,1)} copy(bf16[128,2048]{1,0:T(8,128)(2,1)} %get-tuple-element.23) | data formatting | bytes 1048576

commit v3 on v2

--- a/solution.py
+++ b/solution.py
@@ -315,18 +315,19 @@
     def _():
         cot_keep.wait()
 
+    other = p + 1 - 2 * lax.rem(p, 2)
     cot_copies = [
         remote(
-            cot_all.at[rows_of(p), :],
-            cot_all.at[rows_of(p), :],
-            cot_send.at[d - 1],
-            cot_recv.at[d - 1],
-            {"tp": tp_at(d)},
-        )
-        for d in range(1, n)
+            cot_all.at[rows_of(block), :],
+            cot_all.at[rows_of(block), :],
+            cot_send.at[at],
+            cot_recv.at[at],
+            {"tp": to},
+        )
+        for at, (block, to) in enumerate(((p, tp_at(2)), (p, other), (tp_at(2), other)))
     ]
-    for copy in cot_copies:
-        copy.start()
+    cot_copies[0].start()
+    cot_copies[1].start()
 
     lax.fori_loop(half_blocks, ncb, conv_block, 0)
 
@@ -396,12 +397,14 @@
             first = tuple(entry[mode_rows(k, h), :] for k in range(modes))
             lax.fori_loop(0, L // 2, step, first)
 
+    cot_copies[0].wait_recv()
+    cot_copies[2].start()
     last_state(False)
     forward_states = state_copies(1, state_send, state_recv, 0)
     for copy in forward_states:
         copy.start()
 
-    for copy in cot_copies:
+    for copy in cot_copies[1:]:
         copy.wait_recv()
 
     tile = min(256, C)

time: 141 us -> 140 us (level)
  Pallas kernels: 126 us -> 124 us
    pallas_call x1, Pallas kernels: 126 us -> 124 us  [fused_shards(): pl.pallas_call(functools.partial(fused_kernel, n), out_shape=(jax.ShapeDt...]
where the time goes in v3:
time: 140 us; the launch traced here: 139 us
  Pallas kernels  124 us (89%)
  local copies, waits for them, and re-layouts  13.5 us (10%)
    pallas_call x1, Pallas kernels, fused_shards(): pl.pallas_call(functools.partial(fused_kernel, n), out_shape=(jax.ShapeDt...  124 us
    unnamed x4, local copies, waits for them, and re-layouts  7.31 us

profile of v3, /device:TPU:1, one launch (start us, length us, event | category | flops | bytes accessed | tf_op | source)
XLA Modules:
  0.0 139.2 jit_solution(11222497830791842204)
XLA Ops:
  0.6 1.1 sqrt_multiply_fusion
  1.7 0.7 reshape.24.scaled_ref
  2.4 1.6 %reshape.23.rates_ref = f32[256,128]{1,0:T(8,128)} reshape(f32[16,2048]{1,0:T(8,128)} %param.12) | data formatting | bytes 262144 | tf_op jit(solution)/shard_map/reshape | solution.py:781
  4.0 1.1 broadcast_in_dim.3
  5.1 1.5 %reshape.22.taps_ref = f32[3,7,2048]{2,1,0:T(8,128)} reshape(f32[3,7,128,16]{3,2,1,0:T(8,128)S(1)} %broadcast_in_dim.3) | data formatting | bytes 344064 | tf_op jit(solution)/shard_map/reshape | solution.py:712
  6.5 124.0 %shard_map.119 = (bf16[128,1024]{1,0:T(8,128)(2,1)}, bf16[128,2048]{1,0:T(8,128)(2,1)}, bf16[128,2048]{1,0:T(8,128)(2,1)}, bf16[128,2048]{1,0:T(8,128)(2,1)}, f32[24,128]{1,0:T(8,128)}) custom-call(bf16[128,2048]{1,0:T(8,128)(2,1)} %q_ref.1, bf16[128,2048]{1,0:T(8,128)(2,1)} %k_ref.1, bf16[128,2048]{1,0:T(8,128)(2,1)} %v_ref.1, ...), custom_call_target="tpu_custom_call" | custom-call | tf_op jit(solution)/shard_map/pallas_call | solution.py:718
  130.6 1.3 slice_bitcast_fusion
  131.9 1.7 %copy.17 = bf16[128,1024]{1,0:T(8,128)(2,1)} copy(bf16[128,1024]{1,0:T(8,128)(2,1)} %get-tuple-element.20) | data formatting | bytes 524288
  133.5 1.9 %copy.18 = bf16[128,2048]{1,0:T(8,128)(2,1)} copy(bf16[128,2048]{1,0:T(8,128)(2,1)} %get-tuple-element.21) | data formatting | bytes 1048576
  135.4 1.9 %copy.19 = bf16[128,2048]{1,0:T(8,128)(2,1)} copy(bf16[128,2048]{1,0:T(8,128)(2,1)} %get-tuple-element.22) | data formatting | bytes 1048576
  137.3 1.9 %copy.20 = bf16[128,2048]{1,0:T(8,128)(2,1)} copy(bf16[128,2048]{1,0:T(8,128)(2,1)} %get-tuple-element.23) | data formatting | bytes 1048576
